TPU v7x, 32 devices: a whole 2x2x4 slice. The times are simulated.
32 devices in a mesh: groups: 2 (over x), param: 16 (over z, y, core).
Axes of the slice: x: 2, y: 2, z: 4, core: 2. Of those that a mesh axis runs over, the one named last changes fastest.
Arguments:
- gradients: bfloat16 [1024, 10240], P('groups', 'param'), parts along dimension 0
- proj_matrix: bfloat16 [10240, 8192], P('param')
- train_task: int32 [768], P('groups'), parts along dimension 0, may hold values from 0 to 11, as said below
- val_task: int32 [256], P('groups'), parts along dimension 0, may hold values from 0 to 7, as said below
- task_pairs: int32 [64, 2], P(('groups', 'param')), parts along dimension 0, may hold values from 0 to 11, as said below
- owner_slot: int32 [1024], P('groups'), parts along dimension 0, may hold values from 0 to 511, each once
Outputs:
- unit_rows: bfloat16 [1024, 8192], P(('groups', 'param')), parts along dimension 0
- tiles: float32 [64, 32, 16], P(('groups', 'param')), parts along dimension 0
- scores: float32 [1024], P(('groups', 'param')), parts along dimension 0
There are 2 independent parts, one for each index of `groups`. A program takes and returns all parts, laid end to end along the dimension named above; an argument that names none is the same for every part. Nothing has to cross between parts.
Inputs may be any that keep to these rules, and one draw needn't show every extreme that they name: `train_task`: every training task holds exactly 32 examples. `val_task`: every validation task holds exactly 16 examples. `task_pairs`: column 0 is a training task, column 1 a validation task; every task appears; pairs may repeat.
All inputs are finite; a program needn't handle non-finite values.
Results may differ from a plain program's by a relative error of at most 0.0026.
Values may be sent and summed in bfloat16 or wider, within the bound.
A program may use at most 128 MiB of HBM per device.

v0:
```python
import jax
import jax.numpy as jnp
from jax import lax
from jax.sharding import PartitionSpec as P

TRAIN_TASKS = 12
TRAIN_PER = 32
VAL_TASKS = 8
VAL_PER = 16
TRAIN = 384


epsilon = 1e-06


def shards(gradients, proj_matrix, train_task, val_task, task_pairs, owner_slot):
    total_rows = gradients.shape[0]
    inverse = (
        jnp.zeros((total_rows,), jnp.int32)
        .at[owner_slot]
        .set(jnp.arange(total_rows, dtype=jnp.int32))
    )
    ordered = gradients[inverse]
    owned = lax.psum_scatter(
        jnp.dot(ordered, proj_matrix, preferred_element_type=jnp.float32),
        "param",
        scatter_dimension=0,
        tiled=True,
    )
    squares = jnp.sum(owned * owned, axis=1, keepdims=True)
    unit_rows = (owned * lax.rsqrt(squares + epsilon)).astype(jnp.bfloat16)
    train_rows = jnp.argsort(train_task, stable=True).reshape(TRAIN_TASKS, TRAIN_PER)
    val_order = jnp.argsort(val_task, stable=True).reshape(VAL_TASKS, VAL_PER)
    left_slots = owner_slot[train_rows[task_pairs[:, 0]]]
    val_index = val_order[task_pairs[:, 1]]
    right_slots = owner_slot[val_index + TRAIN]
    every_unit = lax.all_gather(unit_rows, "param", axis=0, tiled=True)
    left_side = every_unit[left_slots]
    right_side = every_unit[right_slots]
    tiles = jnp.einsum("prk,pck->prc", left_side, right_side, preferred_element_type=jnp.float32)
    contrib = jnp.zeros((total_rows,), jnp.float32)
    contrib = contrib.at[left_slots].add(jnp.mean(tiles, axis=2))
    contrib = contrib.at[right_slots].add(jnp.mean(tiles, axis=1))
    scores = lax.psum_scatter(contrib, "param", scatter_dimension=0, tiled=True)
    return (unit_rows, tiles, scores)


def solution(mesh):
    in_specs = (
        P("groups", "param"),
        P("param", None),
        P("groups"),
        P("groups"),
        P(("groups", "param"), None),
        P("groups"),
    )
    out_specs = (
        P(("groups", "param"), None),
        P(("groups", "param"), None, None),
        P(("groups", "param")),
    )
    return jax.shard_map(shards, mesh=mesh, in_specs=in_specs, out_specs=out_specs, check_vma=False)
```

profile of v0, /device:TPU:0, one launch (start us, length us, event | category | flops | bytes accessed | tf_op | source)
XLA Modules:
  0.0 340.1 jit_solution(2842748217591299580)
XLA Ops:
  7.2 0.7 compare_select_fusion.1
  8.0 2.4 scatter_custom_fusion
  10.4 2.0 gather_fusion
  12.5 14.1 %fusion.7 = f32[512,8192]{1,0:T(8,128)} fusion(bf16[512,640]{1,0:T(8,128)(2,1)S(1)} %gather_fusion, bf16[640,8192]{1,0:T(8,128)(2,1)} %param.7), kind=kOutput, calls=%fused_computation.37 | convolution fusion | flops 5368709120 | bytes 27918336 | tf_op jit(solution)/shard_map/dot_general | solution.py:25
  26.6 181.4 %reduce-scatter.2.cloned.1.call-done = f32[32,8192]{1,0:T(8,128)} async-done(((f32[512,8192]{1,0:T(8,128)}), f32[32,8192]{1,0:T(8,128)}) %reduce-scatter.2.cloned.1.call-update) | async-done | bytes 1048592 | tf_op jit(solution)/shard_map/reduce_scatter | solution.py:24
  208.0 1.4 multiply_reduce_fusion
  209.4 2.2 multiply_convert_fusion
  211.6 3.8 %sort.34 = (s32[384]{0:T(512)}, s32[384]{0:T(512)S(1)}) sort(s32[384]{0:T(512)S(1)} %copy-done.3, s32[384]{0:T(512)S(1)} %iota.12), dimensions={0}, to_apply=%region_3.0 | sort | flops 3456 | bytes 6144 | tf_op jit(solution)/shard_map/jit(argsort)/sort | solution.py:32
  215.5 0.2 fusion.1
  215.7 0.6 gather_fusion.1
  216.2 0.1 reshape.97
  216.3 0.8 gather_fusion.2
  217.1 0.1 gather.31
  217.2 0.1 reshape.105
  217.3 2.5 sort.35
  219.8 0.1 reshape.78
  219.9 0.6 gather_fusion.4
  220.5 0.1 reshape.121
  220.6 0.7 gather_fusion.5
  221.3 0.1 gather.35
  221.4 0.1 reshape.129
  221.5 0.6 dynamic-slice
  222.7 63.6 %all-gather.2.cloned.1.call-done = bf16[512,8192]{1,0:T(8,128)(2,1)} async-done(((bf16[32,8192]{1,0:T(8,128)(2,1)}), bf16[512,8192]{1,0:T(8,128)(2,1)}) %all-gather.2.cloned.1.call-update) | async-done | bytes 8388624 | tf_op jit(solution)/shard_map/all_gather | solution.py:37
  286.4 6.6 %gather_fusion.3 = bf16[64,8192]{1,0:T(8,128)(2,1)S(1)} fusion(bf16[512,8192]{1,0:T(8,128)(2,1)} %all-gather.2.cloned.1.call-done, s32[1024]{0:T(1024)S(1)} %pad_clamp_fusion.3), kind=kCustom, calls=%fused_computation.3 | custom fusion | bytes 2097408 | tf_op jit(solution)/shard_map/gather | solution.py:38
  293.0 5.8 %gather_fusion.6 = bf16[32,8192]{1,0:T(8,128)(2,1)S(1)} fusion(bf16[512,8192]{1,0:T(8,128)(2,1)} %all-gather.2.cloned.1.call-done, s32[1024]{0:T(1024)S(1)} %pad_clamp_fusion), kind=kCustom, calls=%fused_computation.6 | custom fusion | bytes 1048704 | tf_op jit(solution)/shard_map/gather | solution.py:39
  298.8 1.0 fusion.6
  299.8 0.1 reshape.147
  299.9 0.1 reshape.155
  300.0 1.0 scatter_custom_fusion.1
  301.0 0.8 scatter_fusion
  301.7 31.0 %all-reduce = f32[512]{0:T(512)S(1)} all-reduce(f32[512]{0:T(512)S(1)} %scatter_fusion), channel_id=3, replica_groups=mesh['groups'=2,'param'=16] {'param'}, use_global_device_ids=true, to_apply=%region_9.10.clone | all-reduce | flops 512 | bytes 4096
  332.7 0.6 dynamic-slice.1
  (34 shorter events, 0.3 us)
Async XLA Ops:
  7.2 3.3 copy-start
  7.2 200.8 %reduce-scatter.2.cloned.1.call-start = ((), (), s32[]{:S(2)}) async-start(), calls=%async_computation.1 | async-start | bytes 17825792 | tf_op jit(solution)/shard_map/reduce_scatter | solution.py:24
  26.5 185.1 %copy-start.3 = (s32[384]{0:T(512)S(1)}, s32[384]{0:T(512)}, u32[]{:S(2)}) copy-start(s32[384]{0:T(512)} %param.8) | copy-start | bytes 4612
  26.6 188.9 %copy-start.2 = (s32[2,2]{1,0:T(2,128)S(1)}, s32[2,2]{1,0:T(2,128)}, u32[]{:S(2)}) copy-start(s32[2,2]{1,0:T(2,128)} %param.10) | copy-start | bytes 52
  26.6 189.8 %copy-start.1 = (s32[512]{0:T(512)S(1)}, s32[512]{0:T(512)}, u32[]{:S(2)}) copy-start(s32[512]{0:T(512)} %param.11) | copy-start | bytes 6148
  26.6 190.7 %copy-start.4 = (s32[128]{0:T(128)S(1)}, s32[128]{0:T(128)}, u32[]{:S(2)}) copy-start(s32[128]{0:T(128)} %param.9) | copy-start | bytes 1540
  26.6 194.9 %copy-start.5 = (u32[32]{0:T(128)S(1)}, u32[32]{0:T(128)}, u32[]{:S(2)}) copy-start(u32[32]{0:T(128)} %constant.31) | copy-start | bytes 388
  26.6 259.8 %all-gather.2.cloned.1.call-start = ((), (), s32[]{:S(2)}) async-start(), calls=%async_computation.2 | async-start | bytes 8912896 | tf_op jit(solution)/shard_map/all_gather | solution.py:37
Sparse Core Ops, SparseCore 0:
  26.7 181.2 reduce-scatter.1
  211.7 74.5 all-gather.1
where the time goes:
time: 340 us
  waiting for transfers between devices  245 us (72%)
  blocking collectives  31 us (9%)
  local copies, waits for them, and re-layouts  21.5 us (6%)
  matrix products  15.1 us (4%)
  between operations  14.8 us (4%)
  other arithmetic  12.6 us (4%)
    reduce_scatter x1, waiting for transfers between devices, shards(): lax.psum_scatter(jnp.dot(ordered, proj_matrix, preferred_element_type=jnp...  181 us
    all_gather x1, waiting for transfers between devices, shards(): every_unit = lax.all_gather(unit_rows, 'param', axis=0, tiled=True)  63.6 us
    unnamed x1, blocking collectives  31 us
    dot_general x1, matrix products, shards(): jnp.dot(ordered, proj_matrix, preferred_element_type=jnp.float32)  14.1 us
  transfers between devices with their start and end apart: 2, of which 2 were waited for; matrix products, arithmetic and copies ran while one was open for 3% of the time, Pallas kernels for 0%

commit v1 on v0

--- a/solution.py
+++ b/solution.py
@@ -1,6 +1,10 @@
+import functools
+
 import jax
 import jax.numpy as jnp
 from jax import lax
+from jax.experimental import pallas as pl
+from jax.experimental.pallas import tpu as pltpu
 from jax.sharding import PartitionSpec as P
 
 TRAIN_TASKS = 12
@@ -8,9 +12,294 @@
 VAL_TASKS = 8
 VAL_PER = 16
 TRAIN = 384
-
+VAL = 128
+CORES = 2
+YS = 2
 
 epsilon = 1e-06
+FULL = 32000.0
+
+
+def row_scale(v):
+    top = jnp.max(jnp.abs(v), axis=1, keepdims=True)
+    return jnp.maximum(top, 1e-30)
+
+
+def to_int16(v, top):
+    return jnp.floor(v * (FULL / top) + 0.5).astype(jnp.int32).astype(jnp.int16)
+
+
+def to_lanes(top):
+    rows = top.shape[0]
+    return jnp.transpose(jnp.broadcast_to(top * (1.0 / FULL), (rows, 128)))[0:1]
+
+
+def to_rows(lanes):
+    return jnp.transpose(jnp.broadcast_to(lanes, (128, 128)))
+
+
+def kernel(
+    zs, g_ref, s_ref, p_ref,
+    unit_ref, gram_ref,
+    p_buf, c_send, c_recv, y_own, y_send, y_recv, ys_send, ys_recv,
+    z_send, z_recv, zs_send, zs_recv, acc, squares, turned,
+    u_send, u_all, g_part, g_recv, g_sum,
+    p_sem, cs_sem, cr_sem, yss_sem, ysr_sem, yds_sem, ydr_sem,
+    zss_sem, zsr_sem, zds_sem, zdr_sem, us_sem, ur_sem, gs_sem, gr_sem, hs_sem, hr_sem,
+):
+    n = zs * YS * CORES
+    chunks, rows, width = acc.shape
+    me = lax.axis_index("param")
+    core = lax.rem(me, CORES)
+    y = lax.rem(lax.div(me, CORES), YS)
+    z = lax.div(me, CORES * YS)
+    sibling = me + 1 - 2 * core
+    y_peer = me + CORES * (1 - 2 * y)
+    half = g_ref.shape[0] // 2
+    quarter = half // 2
+
+    def load(k):
+        return pltpu.make_async_copy(
+            p_ref.at[:, pl.ds(pl.multiple_of(k * width, width), width)], p_buf.at[k], p_sem.at[k])
+
+    def start_load(k, carry):
+        load(k).start()
+        return carry
+
+    lax.fori_loop(0, chunks, start_load, 0)
+
+    barrier = pltpu.get_barrier_semaphore()
+    for j in range(1, n):
+        pl.semaphore_signal(barrier, inc=1, device_id={"param": lax.rem(me + j, n)},
+                            device_id_type=pl.DeviceIdType.MESH)
+    pl.semaphore_wait(barrier, n - 1)
+
+    def remote(src, dst, send, recv, to):
+        return pltpu.make_async_remote_copy(
+            src_ref=src, dst_ref=dst, send_sem=send, recv_sem=recv,
+            device_id={"param": to}, device_id_type=pl.DeviceIdType.MESH)
+
+    def core_copy(k):
+        return remote(c_send.at[k], c_recv.at[k], cs_sem.at[k], cr_sem.at[k], sibling)
+
+    def y_copies(k):
+        return (remote(y_send.at[k], y_recv.at[k], yds_sem.at[k], ydr_sem.at[k], y_peer),
+                remote(ys_send.at[k], ys_recv.at[k], yss_sem.at[k], ysr_sem.at[k], y_peer))
+
+    def z_copies(k, j):
+        zz = lax.rem(z + j, zs)
+        to = zz * (CORES * YS) + y * CORES + core
+        return (remote(z_send.at[k, zz], z_recv.at[k, j - 1], zds_sem.at[k, j - 1],
+                       zdr_sem.at[k, j - 1], to),
+                remote(zs_send.at[k], zs_recv.at[k, j - 1], zss_sem.at[k, j - 1],
+                       zsr_sem.at[k, j - 1], to))
+
+    squares[...] = jnp.zeros_like(squares)
+
+    def step(t, carry):
+        @pl.when(t < chunks)
+        def _():
+            k = t
+            load(k).wait()
+            theirs = g_ref[pl.ds(pl.multiple_of((1 - core) * half, half), half), :]
+            c_send[k] = jnp.dot(theirs, p_buf[k], preferred_element_type=jnp.float32)
+            core_copy(k).start()
+
+        @pl.when(jnp.logical_and(t >= 1, t < chunks + 1))
+        def _():
+            k = t - 1
+            away = pl.multiple_of((1 - y) * quarter, quarter)
+            home = pl.multiple_of(y * quarter, quarter)
+            base = core * half
+            g_away = g_ref[pl.ds(pl.multiple_of(base + away, quarter), quarter), :]
+            g_home = g_ref[pl.ds(pl.multiple_of(base + home, quarter), quarter), :]
+            d_away = jnp.dot(g_away, p_buf[k], preferred_element_type=jnp.float32)
+            d_home = jnp.dot(g_home, p_buf[k], preferred_element_type=jnp.float32)
+            core_copy(k).wait_recv()
+            v = d_away + c_recv[k, pl.ds(away, quarter), :]
+            top = row_scale(v)
+            y_send[k] = to_int16(v, top)
+            ys_send[k] = to_lanes(top)
+            for c in y_copies(k):
+                c.start()
+            y_own[k] = d_home + c_recv[k, pl.ds(home, quarter), :]
+
+        @pl.when(jnp.logical_and(t >= 3, t < chunks + 3))
+        def _():
+            k = t - 3
+            for c in y_copies(k):
+                c.wait_recv()
+            scale = to_rows(ys_recv[k])[:, 0:1]
+            v = y_own[k] + y_recv[k].astype(jnp.int32).astype(jnp.float32) * scale
+            top = row_scale(v)
+            q = to_int16(v, top)
+            z_send[k] = q.reshape(zs, rows, width)
+            zs_send[k] = to_lanes(top)
+            for j in range(1, zs):
+                for c in z_copies(k, j):
+                    c.start()
+            y_own[k] = v
+            acc[k] = y_own[k, pl.ds(pl.multiple_of(z * rows, rows), rows), :]
+
+        @pl.when(t >= 5)
+        def _():
+            k = t - 5
+            v = acc[k]
+            for j in range(1, zs):
+                for c in z_copies(k, j):
+                    c.wait_recv()
+                turned[...] = to_rows(zs_recv[k, j - 1])
+                scale = turned[pl.ds(pl.multiple_of(z * rows, rows), rows), :][:, 0:1]
+                v = v + z_recv[k, j - 1].astype(jnp.int32).astype(jnp.float32) * scale
+            acc[k] = v
+            squares[...] += jnp.sum(v * v, axis=1, keepdims=True)
+
+        return carry
+
+    lax.fori_loop(0, chunks + 5, step, 0)
+
+    factor = lax.rsqrt(squares[...] + epsilon)[:, 0:1]
+    for k in range(chunks):
+        u = (acc[k] * factor).astype(jnp.bfloat16)
+        unit_ref[:, k * width:(k + 1) * width] = u
+        u_send[k] = u
+
+    def u_copy(j):
+        to = lax.rem(me + j, n)
+        return remote(u_send.at[to], u_all.at[me], us_sem.at[j - 1], ur_sem.at[j - 1], to)
+
+    for j in range(1, n):
+        u_copy(j).start()
+    u_all[me] = u_send[me]
+
+    def drain(k, carry):
+        core_copy(k).wait_send()
+        for c in y_copies(k):
+            c.wait_send()
+        for j in range(1, zs):
+            for c in z_copies(k, j):
+                c.wait_send()
+        return carry
+
+    lax.fori_loop(0, chunks, drain, 0)
+    for j in range(1, n):
+        u_copy(j).wait()
+
+    whole = u_all[...].reshape(n * rows, width)
+    ordered = jnp.dot(s_ref[...], whole, preferred_element_type=jnp.float32).astype(jnp.bfloat16)
+    gram = lax.dot_general(ordered[:TRAIN], ordered[TRAIN:], (((1,), (1,)), ((), ())),
+                           preferred_element_type=jnp.float32)
+    g_part[...] = gram.reshape(g_part.shape)
+
+    def g_copy(j):
+        to = lax.rem(me + j, n)
+        return remote(g_part.at[to], g_recv.at[j - 1], gs_sem.at[j - 1], gr_sem.at[j - 1], to)
+
+    for j in range(1, n):
+        g_copy(j).start()
+    total = g_part[me]
+    for j in range(1, n):
+        g_copy(j).wait_recv()
+        total = total + g_recv[j - 1]
+    g_sum[...] = total
+
+    def h_copy(j):
+        to = lax.rem(me + j, n)
+        return remote(g_sum, gram_ref.at[me], hs_sem.at[j - 1], hr_sem.at[j - 1], to)
+
+    for j in range(1, n):
+        h_copy(j).start()
+    gram_ref[me] = total
+    for j in range(1, n):
+        g_copy(j).wait_send()
+        h_copy(j).wait()
+
+
+def project(n, ordered, select, proj_matrix):
+    zs = n // (CORES * YS)
+    total, depth = ordered.shape
+    cols = proj_matrix.shape[1]
+    rows, width, chunks = total // n, cols // n, n
+    half, quarter = total // 2, total // 4
+    f32, bf16, i16 = jnp.float32, jnp.bfloat16, jnp.int16
+    dma = pltpu.SemaphoreType.DMA
+    part = TRAIN // n
+    vmem = pl.BlockSpec(memory_space=pltpu.VMEM)
+    return pl.pallas_call(
+        functools.partial(kernel, zs),
+        out_shape=(jax.ShapeDtypeStruct((rows, cols), bf16),
+                   jax.ShapeDtypeStruct((n, part, VAL), f32)),
+        in_specs=[vmem, vmem, pl.BlockSpec(memory_space=pl.ANY)],
+        out_specs=(vmem, vmem),
+        scratch_shapes=[
+            pltpu.VMEM((chunks, depth, width), bf16),
+            pltpu.VMEM((chunks, half, width), f32),
+            pltpu.VMEM((chunks, half, width), f32),
+            pltpu.VMEM((chunks, quarter, width), f32),
+            pltpu.VMEM((chunks, quarter, width), i16),
+            pltpu.VMEM((chunks, quarter, width), i16),
+            pltpu.VMEM((chunks, 1, quarter), f32),
+            pltpu.VMEM((chunks, 1, quarter), f32),
+            pltpu.VMEM((chunks, zs, rows, width), i16),
+            pltpu.VMEM((chunks, zs - 1, rows, width), i16),
+            pltpu.VMEM((chunks, 1, quarter), f32),
+            pltpu.VMEM((chunks, zs - 1, 1, quarter), f32),
+            pltpu.VMEM((chunks, rows, width), f32),
+            pltpu.VMEM((rows, 128), f32),
+            pltpu.VMEM((128, 128), f32),
+            pltpu.VMEM((n, rows, width), bf16),
+            pltpu.VMEM((n, rows, width), bf16),
+            pltpu.VMEM((n, part, VAL), f32),
+            pltpu.VMEM((n - 1, part, VAL), f32),
+            pltpu.VMEM((part, VAL), f32),
+            dma((chunks,)),
+            dma((chunks,)), dma((chunks,)),
+            dma((chunks,)), dma((chunks,)), dma((chunks,)), dma((chunks,)),
+            dma((chunks, zs - 1)), dma((chunks, zs - 1)),
+            dma((chunks, zs - 1)), dma((chunks, zs - 1)),
+            dma((n - 1,)), dma((n - 1,)), dma((n - 1,)), dma((n - 1,)),
+            dma((n - 1,)), dma((n - 1,)),
+        ],
+        compiler_params=pltpu.CompilerParams(
+            collective_id=0, has_side_effects=True, vmem_limit_bytes=60 * 2**20),
+        cost_estimate=pl.CostEstimate(
+            flops=2 * total * depth * cols, bytes_accessed=2 * depth * cols, transcendentals=0),
+    )(ordered, select, proj_matrix)
+
+
+def fused(n, gradients, proj_matrix, train_task, val_task, task_pairs, owner_slot):
+    total = gradients.shape[0]
+    rows = total // n
+    zs = n // (CORES * YS)
+    me = lax.axis_index("param")
+    index = jnp.arange(total, dtype=jnp.int32)
+
+    def place(task, per):
+        i = jnp.arange(task.shape[0], dtype=jnp.int32)
+        before = (task[None, :] == task[:, None]) & (i[None, :] < i[:, None])
+        return task * per + jnp.sum(before.astype(jnp.int32), axis=1)
+
+    spot = jnp.concatenate([place(train_task, TRAIN_PER), place(val_task, VAL_PER) + TRAIN])
+    owns = owner_slot[None, :] == index[:, None]
+    inverse = jnp.sum(jnp.where(owns, index[None, :], 0), axis=1)
+    spot_of_slot = jnp.sum(jnp.where(owns, spot[None, :], 0), axis=1)
+    select = (spot_of_slot[None, :] == index[:, None]).astype(jnp.bfloat16)
+    order = inverse.reshape(zs, YS, CORES, rows).transpose(2, 1, 0, 3).reshape(total)
+    every_pair = lax.all_gather(task_pairs, "param", axis=0, tiled=True)
+    unit_rows, gram = project(n, gradients[order], select, proj_matrix)
+    gram = gram.reshape(TRAIN, VAL)
+    blocks = gram.reshape(TRAIN_TASKS, TRAIN_PER, VAL_TASKS, VAL_PER)
+    tiles = blocks[task_pairs[:, 0], :, task_pairs[:, 1], :]
+    a = jnp.arange(TRAIN, dtype=jnp.int32) // TRAIN_PER
+    b = jnp.arange(VAL, dtype=jnp.int32) // VAL_PER
+    hits = (every_pair[:, 0, None, None] == a[None, :, None]) & (
+        every_pair[:, 1, None, None] == b[None, None, :])
+    weighted = gram * jnp.sum(hits.astype(jnp.float32), axis=0)
+    sums = jnp.concatenate([
+        jnp.sum(weighted, axis=1) * (1.0 / VAL_PER), jnp.sum(weighted, axis=0) * (1.0 / TRAIN_PER)])
+    mine = lax.dynamic_slice(spot_of_slot, (me * rows,), (rows,))
+    scores = jnp.sum(jnp.where(mine[:, None] == index[None, :], sums[None, :], 0.0), axis=1)
+    return (unit_rows, tiles, scores)
 
 
 def shards(gradients, proj_matrix, train_task, val_task, task_pairs, owner_slot):
@@ -59,4 +348,6 @@
         P(("groups", "param"), None, None),
         P(("groups", "param")),
     )
-    return jax.shard_map(shards, mesh=mesh, in_specs=in_specs, out_specs=out_specs, check_vma=False)
+    n = mesh.shape["param"]
+    body = functools.partial(fused, n) if n == 16 else shards
+    return jax.shard_map(body, mesh=mesh, in_specs=in_specs, out_specs=out_specs, check_vma=False)

time: 340 us -> 129 us (0.38)
  waiting for transfers between devices: 245 us -> 0 us
  Pallas kernels: 0 us -> 90.7 us
  matrix products: 15.1 us -> 0 us
  local copies, waits for them, and re-layouts: 21.5 us -> 7.06 us
  between operations: 14.8 us -> 0.75 us
  blocking collectives: 31 us -> 20.5 us
    reduce_scatter x1 -> x0, waiting for transfers between devices: 181 us -> none  [shards(): lax.psum_scatter(jnp.dot(ordered, proj_matrix, preferred_element_type=jnp...]
    pallas_call x0 -> x1, Pallas kernels: none -> 90.7 us  [project(): pl.pallas_call(functools.partial(kernel, zs), out_shape=(jax.ShapeDtypeSt...]
    all_gather x1 -> x0, waiting for transfers between devices: 63.6 us -> none  [shards(): every_unit = lax.all_gather(unit_rows, 'param', axis=0, tiled=True)]
    unnamed x1 -> x0, blocking collectives: 31 us -> none
    all_gather x0 -> x1, blocking collectives: none -> 20.5 us  [fused(): every_pair = lax.all_gather(task_pairs, 'param', axis=0, tiled=True)]
    dot_general x2 -> x0, matrix products: 15.1 us -> none  [the longest x1 14.1 us: shards(): jnp.dot(ordered, proj_matrix, preferred_element_type=jnp.float32)]
    gather x9 -> x2, local copies, waits for them, and re-layouts: 17.2 us -> 3.86 us  [the longest x1 2.69 us: fused(): unit_rows, gram = project(n, gradients[order], select, proj_matrix)]
    sort x2 -> x0, other arithmetic: 6.31 us -> none  [the longest x1 3.77 us: shards(): jnp.argsort(train_task, stable=True).reshape(TRAIN_TASKS, TRAIN_PER)]
  transfers between devices with their start and end apart: 2 -> 0, of which waited for: 2 -> 0; matrix products, arithmetic and copies ran while one was open for 3% -> 0% of each run, Pallas kernels for 0% -> 0%
where the time goes in v1:
time: 129 us
  Pallas kernels  90.7 us (70%)
  blocking collectives  20.5 us (16%)
  other arithmetic  9.7 us (8%)
  local copies, waits for them, and re-layouts  7.06 us (5%)
    pallas_call x1, Pallas kernels, project(): pl.pallas_call(functools.partial(kernel, zs), out_shape=(jax.ShapeDtypeSt...  90.7 us
    all_gather x1, blocking collectives, fused(): every_pair = lax.all_gather(task_pairs, 'param', axis=0, tiled=True)  20.5 us
    gather x1, local copies, waits for them, and re-layouts, fused(): unit_rows, gram = project(n, gradients[order], select, proj_matrix)  2.69 us

profile of v1, /device:TPU:0, one launch (start us, length us, event | category | flops | bytes accessed | tf_op | source)
XLA Modules:
  0.0 128.7 jit_solution(18304946998030118423)
XLA Ops:
  0.6 0.0 copy-start
  0.6 1.0 convert_reduce_fusion.1
  1.6 0.7 multiply_add_fusion
  2.3 0.9 convert_reduce_fusion.2
  3.2 0.7 add_add_fusion
  3.9 1.0 select_reduce_fusion
  5.0 0.9 fusion.s_ref
  5.9 0.1 reshape.147
  6.0 0.1 reshape.148
  6.1 0.0 copy-done
  6.1 2.7 %gather_fusion = bf16[512,640]{1,0:T(8,128)(2,1)} fusion(bf16[512,640]{1,0:T(8,128)(2,1)S(1)} %copy-done, s32[1024]{0:T(1024)S(1)} %pad_clamp_fusion), kind=kCustom, calls=%fused_computation | custom fusion | bytes 1312768 | tf_op jit(solution)/shard_map/gather | solution.py:289
  8.8 0.0 copy-start.2
  8.8 90.7 %shard_map.85 = (bf16[32,8192]{1,0:T(8,128)(2,1)}, f32[16,24,128]{2,1,0:T(8,128)}) custom-call(bf16[512,640]{1,0:T(8,128)(2,1)} %gather_fusion, bf16[512,512]{1,0:T(8,128)(2,1)} %fusion.s_ref, bf16[640,8192]{1,0:T(8,128)(2,1)} %p_ref.1), custom_call_target="tpu_custom_call" | custom-call | flops 5368709120 | bytes 10485760 | tf_op jit(solution)/shard_map/pallas_call | solution.py:228
  99.5 0.0 copy-done.2
  99.5 20.5 %all-gather = s32[16,2,2]{2,1,0:T(2,128)S(1)} all-gather(s32[1,2,2]{2,1,0:T(2,128)S(1)} %bitcast.10), channel_id=1, replica_groups=mesh['groups'=2,'param'=16] {'param'}, dimensions={0}, use_global_device_ids=true | all-gather | bytes 272 | tf_op jit(solution)/shard_map/all_gather | solution.py:288
  120.0 0.1 fusion.12
  120.0 0.1 copy.22
  120.1 0.1 broadcast_compare_fusion
  120.2 0.1 copy.23
  120.3 0.1 broadcast_compare_fusion.1
  120.4 2.3 %convert_reduce_fusion = f32[384,128]{1,0:T(8,128)S(1)} fusion(pred[32,128]{1,0:T(8,128)(4,1)S(1)} %broadcast_compare_fusion.1, pred[32,384]{1,0:T(8,128)(4,1)S(1)} %broadcast_compare_fusion), kind=kLoop, calls=%fused_computation.2 | loop fusion | flops 4669440 | bytes 212992 | tf_op jit(solution)/shard_map/reduce_sum | solution.py:297
  122.7 1.1 multiply_reduce_fusion.1
  123.8 0.1 mul.43
  123.9 0.1 dynamic_slice.3
  124.0 0.7 select_reduce_fusion.2
  124.7 1.4 %reshape_reshape.3 = f32[12,32,8,16]{3,2,1,0:T(8,128)S(1)} reshape(f32[16,24,128]{2,1,0:T(8,128)} %get-tuple-element.6) | data formatting | bytes 393216 | tf_op jit(solution)/shard_map/reshape;reshape | solution.py:291
  126.0 0.0 copy-start.1
  126.1 0.5 copy.19
  126.5 0.2 fusion.11
  126.7 1.2 gather_fusion.1
  127.9 0.0 copy-done.1
  127.9 0.8 copy.25
  (9 shorter events, 0.1 us)
Async XLA Ops:
  0.6 5.5 %copy-start = (bf16[512,640]{1,0:T(8,128)(2,1)S(1)}, bf16[512,640]{1,0:T(8,128)(2,1)}, u32[]{:S(2)}) copy-start(bf16[512,640]{1,0:T(8,128)(2,1)} %param.6) | copy-start | bytes 1966084
  8.8 90.7 %copy-start.2 = (s32[2,2]{1,0:T(2,128)S(1)}, s32[2,2]{1,0:T(2,128)}, u32[]{:S(2)}) copy-start(s32[2,2]{1,0:T(2,128)} %param.10) | copy-start | bytes 52
  126.0 1.8 %copy-start.1 = (bf16[32,8192]{1,0:T(8,128)(2,1)S(1)}, bf16[32,8192]{1,0:T(8,128)(2,1)}, u32[]{:S(2)}) copy-start(bf16[32,8192]{1,0:T(8,128)(2,1)} %get-tuple-element.16) | copy-start | bytes 1572868

commit v2 on v1

--- a/solution.py
+++ b/solution.py
@@ -39,13 +39,14 @@
 
 
 def kernel(
-    zs, g_ref, s_ref, p_ref,
-    unit_ref, gram_ref,
+    zs, pairs_ref, g_in, owner_ref, train_ref, val_ref, p_ref,
+    unit_ref, tile_ref, score_ref,
+    g_ref, s_ref, gram_ref, count_own, count_recv,
     p_buf, c_send, c_recv, y_own, y_send, y_recv, ys_send, ys_recv,
     z_send, z_recv, zs_send, zs_recv, acc, squares, turned,
     u_send, u_all, g_part, g_recv, g_sum,
     p_sem, cs_sem, cr_sem, yss_sem, ysr_sem, yds_sem, ydr_sem,
-    zss_sem, zsr_sem, zds_sem, zdr_sem, us_sem, ur_sem, gs_sem, gr_sem, hs_sem, hr_sem,
+    zss_sem, zsr_sem, zds_sem, zdr_sem, us_sem, ur_sem, gs_sem, gr_sem, hs_sem, hr_sem, ns_sem, nr_sem,
 ):
     n = zs * YS * CORES
     chunks, rows, width = acc.shape
@@ -74,10 +75,56 @@
                             device_id_type=pl.DeviceIdType.MESH)
     pl.semaphore_wait(barrier, n - 1)
 
+    def number(shape, axis):
+        return lax.broadcasted_iota(jnp.int32, shape, axis)
+
+    def ones_where(condition):
+        return jnp.where(condition, 1.0, 0.0)
+
     def remote(src, dst, send, recv, to):
         return pltpu.make_async_remote_copy(
             src_ref=src, dst_ref=dst, send_sem=send, recv_sem=recv,
             device_id={"param": to}, device_id_type=pl.DeviceIdType.MESH)
+
+    count = jnp.zeros(count_own.shape, jnp.float32)
+    for i in range(pairs_ref.shape[0]):
+        count = count + ones_where(
+            (number(count.shape, 0) == pairs_ref[i, 0])
+            & (number(count.shape, 1) >> (VAL_PER.bit_length() - 1) == pairs_ref[i, 1]))
+    count_own[...] = count
+
+    def n_copy(j):
+        to = lax.rem(me + j, n)
+        return remote(count_own, count_recv.at[j - 1], ns_sem.at[j - 1], nr_sem.at[j - 1], to)
+
+    for j in range(1, n):
+        n_copy(j).start()
+
+    total_rows = g_in.shape[0]
+    line = number((total_rows, 1), 0)
+    bit = rows.bit_length() - 1
+    zbit = zs.bit_length() - 1
+    slot = (((line >> bit) & (zs - 1)) * 4 + ((line >> (bit + zbit)) & 1) * 2
+            + (line >> (bit + zbit + 1))) * rows + (line & (rows - 1))
+    pick = ones_where(slot == owner_ref[...]).astype(jnp.bfloat16)
+    g_ref[...] = jnp.dot(pick, g_in[...], preferred_element_type=jnp.float32).astype(jnp.bfloat16)
+
+    def place(task, per, tasks):
+        size = task.shape[1]
+        held = ones_where(number((tasks, size), 0) == task)
+        below = ones_where(number((size, size), 0) < number((size, size), 1))
+        before = jnp.dot(held.astype(jnp.bfloat16), below.astype(jnp.bfloat16),
+                         preferred_element_type=jnp.float32)
+        rank = jnp.sum(held * before, axis=0, keepdims=True).astype(jnp.int32)
+        return task * per + rank
+
+    spot_t = place(train_ref[...], TRAIN_PER, 16)
+    spot_v = place(val_ref[...], VAL_PER, 16) + TRAIN
+    by_slot = ones_where(line == owner_ref[...]).astype(jnp.bfloat16)
+    spot = jnp.concatenate([spot_t, spot_v], axis=1)
+    by_spot = ones_where(line == spot).astype(jnp.bfloat16)
+    s_ref[...] = lax.dot_general(by_spot, by_slot, (((1,), (1,)), ((), ())),
+                                 preferred_element_type=jnp.float32).astype(jnp.bfloat16)
 
     def core_copy(k):
         return remote(c_send.at[k], c_recv.at[k], cs_sem.at[k], cr_sem.at[k], sibling)
@@ -213,25 +260,55 @@
     for j in range(1, n):
         g_copy(j).wait_send()
         h_copy(j).wait()
-
-
-def project(n, ordered, select, proj_matrix):
+        n_copy(j).wait()
+
+    count = count_own[...]
+    for j in range(1, n):
+        count = count + count_recv[j - 1]
+    gram = gram_ref[...].reshape(TRAIN_TASKS, TRAIN_PER, VAL)
+    weighted = (gram * count[:TRAIN_TASKS][:, None, :]).reshape(TRAIN, VAL)
+    by_train = jnp.sum(weighted, axis=1, keepdims=True) * (1.0 / VAL_PER)
+    by_val = jnp.sum(weighted, axis=0, keepdims=True) * (1.0 / TRAIN_PER)
+    by_val = jnp.transpose(jnp.broadcast_to(by_val, (VAL, VAL)))[:, 0:1]
+    score_ref[...] = (
+        jnp.sum(s_ref[:TRAIN, :].astype(jnp.float32) * by_train, axis=0, keepdims=True)
+        + jnp.sum(s_ref[TRAIN:, :].astype(jnp.float32) * by_val, axis=0, keepdims=True))
+    whole_gram = gram_ref[...].reshape(TRAIN_TASKS, TRAIN_PER, VAL)
+    for i in range(pairs_ref.shape[0]):
+        left = jnp.zeros((TRAIN_PER, VAL), jnp.float32)
+        for a in range(TRAIN_TASKS):
+            left = left + jnp.where(pairs_ref[i, 0] == a, whole_gram[a], 0.0)
+        chosen = ones_where(number((VAL, VAL_PER), 0)
+                            == number((VAL, VAL_PER), 1) + pairs_ref[i, 1] * VAL_PER)
+        tile_ref[i] = jnp.dot(left, chosen, preferred_element_type=jnp.float32,
+                              precision=lax.Precision.HIGHEST)
+
+
+def project(n, gradients, proj_matrix, train_task, val_task, task_pairs, owner_slot):
     zs = n // (CORES * YS)
-    total, depth = ordered.shape
+    total, depth = gradients.shape
     cols = proj_matrix.shape[1]
     rows, width, chunks = total // n, cols // n, n
     half, quarter = total // 2, total // 4
     f32, bf16, i16 = jnp.float32, jnp.bfloat16, jnp.int16
     dma = pltpu.SemaphoreType.DMA
     part = TRAIN // n
+    pairs = task_pairs.shape[0]
     vmem = pl.BlockSpec(memory_space=pltpu.VMEM)
     return pl.pallas_call(
         functools.partial(kernel, zs),
         out_shape=(jax.ShapeDtypeStruct((rows, cols), bf16),
-                   jax.ShapeDtypeStruct((n, part, VAL), f32)),
-        in_specs=[vmem, vmem, pl.BlockSpec(memory_space=pl.ANY)],
-        out_specs=(vmem, vmem),
+                   jax.ShapeDtypeStruct((pairs, TRAIN_PER, VAL_PER), f32),
+                   jax.ShapeDtypeStruct((1, total), f32)),
+        in_specs=[pl.BlockSpec(memory_space=pltpu.SMEM), vmem, vmem, vmem, vmem,
+                  pl.BlockSpec(memory_space=pl.ANY)],
+        out_specs=(vmem, vmem, vmem),
         scratch_shapes=[
+            pltpu.VMEM((total, depth), bf16),
+            pltpu.VMEM((total, total), bf16),
+            pltpu.VMEM((n, part, VAL), f32),
+            pltpu.VMEM((16, VAL), f32),
+            pltpu.VMEM((n - 1, 16, VAL), f32),
             pltpu.VMEM((chunks, depth, width), bf16),
             pltpu.VMEM((chunks, half, width), f32),
             pltpu.VMEM((chunks, half, width), f32),
@@ -258,48 +335,22 @@
             dma((chunks, zs - 1)), dma((chunks, zs - 1)),
             dma((chunks, zs - 1)), dma((chunks, zs - 1)),
             dma((n - 1,)), dma((n - 1,)), dma((n - 1,)), dma((n - 1,)),
-            dma((n - 1,)), dma((n - 1,)),
+            dma((n - 1,)), dma((n - 1,)), dma((n - 1,)), dma((n - 1,)),
         ],
         compiler_params=pltpu.CompilerParams(
             collective_id=0, has_side_effects=True, vmem_limit_bytes=60 * 2**20),
         cost_estimate=pl.CostEstimate(
             flops=2 * total * depth * cols, bytes_accessed=2 * depth * cols, transcendentals=0),
-    )(ordered, select, proj_matrix)
+    )(task_pairs, gradients, owner_slot.reshape(1, -1), train_task.reshape(1, -1),
+      val_task.reshape(1, -1), proj_matrix)
 
 
 def fused(n, gradients, proj_matrix, train_task, val_task, task_pairs, owner_slot):
-    total = gradients.shape[0]
-    rows = total // n
-    zs = n // (CORES * YS)
-    me = lax.axis_index("param")
-    index = jnp.arange(total, dtype=jnp.int32)
-
-    def place(task, per):
-        i = jnp.arange(task.shape[0], dtype=jnp.int32)
-        before = (task[None, :] == task[:, None]) & (i[None, :] < i[:, None])
-        return task * per + jnp.sum(before.astype(jnp.int32), axis=1)
-
-    spot = jnp.concatenate([place(train_task, TRAIN_PER), place(val_task, VAL_PER) + TRAIN])
-    owns = owner_slot[None, :] == index[:, None]
-    inverse = jnp.sum(jnp.where(owns, index[None, :], 0), axis=1)
-    spot_of_slot = jnp.sum(jnp.where(owns, spot[None, :], 0), axis=1)
-    select = (spot_of_slot[None, :] == index[:, None]).astype(jnp.bfloat16)
-    order = inverse.reshape(zs, YS, CORES, rows).transpose(2, 1, 0, 3).reshape(total)
-    every_pair = lax.all_gather(task_pairs, "param", axis=0, tiled=True)
-    unit_rows, gram = project(n, gradients[order], select, proj_matrix)
-    gram = gram.reshape(TRAIN, VAL)
-    blocks = gram.reshape(TRAIN_TASKS, TRAIN_PER, VAL_TASKS, VAL_PER)
-    tiles = blocks[task_pairs[:, 0], :, task_pairs[:, 1], :]
-    a = jnp.arange(TRAIN, dtype=jnp.int32) // TRAIN_PER
-    b = jnp.arange(VAL, dtype=jnp.int32) // VAL_PER
-    hits = (every_pair[:, 0, None, None] == a[None, :, None]) & (
-        every_pair[:, 1, None, None] == b[None, None, :])
-    weighted = gram * jnp.sum(hits.astype(jnp.float32), axis=0)
-    sums = jnp.concatenate([
-        jnp.sum(weighted, axis=1) * (1.0 / VAL_PER), jnp.sum(weighted, axis=0) * (1.0 / TRAIN_PER)])
-    mine = lax.dynamic_slice(spot_of_slot, (me * rows,), (rows,))
-    scores = jnp.sum(jnp.where(mine[:, None] == index[None, :], sums[None, :], 0.0), axis=1)
-    return (unit_rows, tiles, scores)
+    rows = gradients.shape[0] // n
+    unit_rows, tiles, scores = project(
+        n, gradients, proj_matrix, train_task, val_task, task_pairs, owner_slot)
+    mine = lax.dynamic_slice(scores, (0, lax.axis_index("param") * rows), (1, rows))
+    return (unit_rows, tiles, mine.reshape(rows))
 
 
 def shards(gradients, proj_matrix, train_task, val_task, task_pairs, owner_slot):

time: 129 us -> 99 us (0.77)
  blocking collectives: 20.5 us -> 0 us
  other arithmetic: 9.7 us -> 0 us
  Pallas kernels: 90.7 us -> 92.3 us
  local copies, waits for them, and re-layouts: 7.06 us -> 5.77 us
    all_gather x1 -> x0, blocking collectives: 20.5 us -> none  [fused(): every_pair = lax.all_gather(task_pairs, 'param', axis=0, tiled=True)]
    reduce_sum x6 -> x0, other arithmetic: 7.02 us -> none  [the longest x1 2.31 us: fused(): weighted = gram * jnp.sum(hits.astype(jnp.float32), axis=0)]
    gather x2 -> x0, local copies, waits for them, and re-layouts: 3.86 us -> none  [the longest x1 2.69 us: fused(): unit_rows, gram = project(n, gradients[order], select, proj_matrix)]
    unnamed x9 -> x2, local copies, waits for them, and re-layouts: 0.96 us -> 3.3 us
    reshape x2, local copies, waits for them, and re-layouts: 0.17 us -> 2.47 us  [the longest x1 1.25 us: project(): train_task.reshape(1, -1)]
    another operation x2 -> x0, local copies, waits for them, and re-layouts: 1.83 us -> none  [fused(): blocks = gram.reshape(TRAIN_TASKS, TRAIN_PER, VAL_TASKS, VAL_PER)]
    pallas_call x1, Pallas kernels: 90.7 us -> 92.3 us  [project(): pl.pallas_call(functools.partial(kernel, zs), out_shape=(jax.ShapeDtypeSt...]
    add x2 -> x0, other arithmetic: 1.36 us -> none  [the longest x1 0.69 us: place(): return task * per + jnp.sum(before.astype(jnp.int32), axis=1)]
where the time goes in v2:
time: 99 us; the launch traced here: 98.7 us
  Pallas kernels  92.3 us (93%)
  local copies, waits for them, and re-layouts  5.77 us (6%)
    pallas_call x1, Pallas kernels, project(): pl.pallas_call(functools.partial(kernel, zs), out_shape=(jax.ShapeDtypeSt...  92.3 us
    unnamed x2, local copies, waits for them, and re-layouts  3.3 us

profile of v2, /device:TPU:0, one launch (start us, length us, event | category | flops | bytes accessed | tf_op | source)
XLA Modules:
  0.0 98.7 jit_solution(9255239001352008823)
XLA Ops:
  0.6 1.2 %reshape.19.train_ref = s32[1,384]{1,0:T(1,128)} reshape(s32[384]{0:T(512)} %param.8) | data formatting | bytes 3072 | tf_op jit(solution)/shard_map/reshape | solution.py:344
  1.9 92.3 %shard_map.85 = (bf16[32,8192]{1,0:T(8,128)(2,1)}, f32[2,32,16]{2,1,0:T(8,128)}, f32[1,512]{1,0:T(1,128)}) custom-call(s32[2,2]{1,0:T(2,128)} %pairs_ref.1, bf16[512,640]{1,0:T(8,128)(2,1)} %g_in.1, s32[1,512]{1,0:T(1,128)} %bitcast.4, s32[1,384]{1,0:T(1,128)} %reshape.19.train_ref, s32[1,128]{1,0:T(1,128)} %bitcast.5, bf16[640,8192]{1,0:T(8,128)(2,1)} %p_ref.1), custom_call_target="tpu_custom_call" | custom-call | flops 5368709120 | bytes 10485760 | tf_op jit(solution)/shard_map/pallas_call | solution.py:298
  94.2 1.2 %dynamic-slice_bitcast_fusion = f32[32]{0:T(128)} fusion(f32[1,512]{1,0:T(1,128)} %get-tuple-element.8, s32[]{:T(128)S(6)} %select_n.3), kind=kLoop, calls=%fused_computation | loop fusion | bytes 260 | tf_op jit(solution)/shard_map/reshape | solution.py:353
  95.4 1.4 %copy.9 = f32[2,32,16]{1,2,0:T(8,128)} copy(f32[2,32,16]{2,1,0:T(8,128)} %get-tuple-element.10) | data formatting | bytes 8192
  96.9 1.9 %copy.11 = bf16[32,8192]{1,0:T(8,128)(2,1)} copy(bf16[32,8192]{1,0:T(8,128)(2,1)} %get-tuple-element.15) | data formatting | bytes 1048576

commit v3 on v2

--- a/solution.py
+++ b/solution.py
@@ -43,10 +43,10 @@
     unit_ref, tile_ref, score_ref,
     g_ref, s_ref, gram_ref, count_own, count_recv,
     p_buf, c_send, c_recv, y_own, y_send, y_recv, ys_send, ys_recv,
-    z_send, z_recv, zs_send, zs_recv, acc, squares, turned,
+    z_own, z_send, z_recv, zs_send, zs_recv, w_send, w_recv, ws_send, ws_recv, acc, squares, turned,
     u_send, u_all, g_part, g_recv, g_sum,
     p_sem, cs_sem, cr_sem, yss_sem, ysr_sem, yds_sem, ydr_sem,
-    zss_sem, zsr_sem, zds_sem, zdr_sem, us_sem, ur_sem, gs_sem, gr_sem, hs_sem, hr_sem, ns_sem, nr_sem,
+    zss_sem, zsr_sem, zds_sem, zdr_sem, wss_sem, wsr_sem, wds_sem, wdr_sem, us_sem, ur_sem, gs_sem, gr_sem, hs_sem, hr_sem, ns_sem, nr_sem,
 ):
     n = zs * YS * CORES
     chunks, rows, width = acc.shape
@@ -56,8 +56,22 @@
     z = lax.div(me, CORES * YS)
     sibling = me + 1 - 2 * core
     y_peer = me + CORES * (1 - 2 * y)
-    half = g_ref.shape[0] // 2
+    near = lax.rem(z, 2)
+    far = lax.div(z, 2)
+    z_peer = me + CORES * YS * (1 - 2 * near)
+    w_peer = me + CORES * YS * 2 * (1 - 2 * far)
+    half = g_in.shape[0] // 2
     quarter = half // 2
+    eighth = quarter // 2
+
+    def swapped(k):
+        return lax.rem(k, 2)
+
+    def first(k):
+        return y + (near - y) * swapped(k)
+
+    def second(k):
+        return near + (y - near) * swapped(k)
 
     def load(k):
         return pltpu.make_async_copy(
@@ -103,11 +117,14 @@
     total_rows = g_in.shape[0]
     line = number((total_rows, 1), 0)
     bit = rows.bit_length() - 1
-    zbit = zs.bit_length() - 1
-    slot = (((line >> bit) & (zs - 1)) * 4 + ((line >> (bit + zbit)) & 1) * 2
-            + (line >> (bit + zbit + 1))) * rows + (line & (rows - 1))
-    pick = ones_where(slot == owner_ref[...]).astype(jnp.bfloat16)
-    g_ref[...] = jnp.dot(pick, g_in[...], preferred_element_type=jnp.float32).astype(jnp.bfloat16)
+    for i in range(2):
+        b_first = (line >> (bit + 2)) & 1
+        b_second = (line >> (bit + 1)) & 1
+        line_y, line_near = (b_first, b_second) if i == 0 else (b_second, b_first)
+        slot = (((line >> bit) & 1) * 8 + line_near * 4 + line_y * 2
+                + (line >> (bit + 3))) * rows + (line & (rows - 1))
+        pick = ones_where(slot == owner_ref[...]).astype(jnp.bfloat16)
+        g_ref[i] = jnp.dot(pick, g_in[...], preferred_element_type=jnp.float32).astype(jnp.bfloat16)
 
     def place(task, per, tasks):
         size = task.shape[1]
@@ -118,7 +135,8 @@
         rank = jnp.sum(held * before, axis=0, keepdims=True).astype(jnp.int32)
         return task * per + rank
 
-    spot_t = place(train_ref[...], TRAIN_PER, 16)
+    train = jnp.concatenate([train_ref[i:i + 1] for i in range(train_ref.shape[0])], axis=1)
+    spot_t = place(train, TRAIN_PER, 16)
     spot_v = place(val_ref[...], VAL_PER, 16) + TRAIN
     by_slot = ones_where(line == owner_ref[...]).astype(jnp.bfloat16)
     spot = jnp.concatenate([spot_t, spot_v], axis=1)
@@ -130,16 +148,18 @@
         return remote(c_send.at[k], c_recv.at[k], cs_sem.at[k], cr_sem.at[k], sibling)
 
     def y_copies(k):
-        return (remote(y_send.at[k], y_recv.at[k], yds_sem.at[k], ydr_sem.at[k], y_peer),
-                remote(ys_send.at[k], ys_recv.at[k], yss_sem.at[k], ysr_sem.at[k], y_peer))
-
-    def z_copies(k, j):
-        zz = lax.rem(z + j, zs)
-        to = zz * (CORES * YS) + y * CORES + core
-        return (remote(z_send.at[k, zz], z_recv.at[k, j - 1], zds_sem.at[k, j - 1],
-                       zdr_sem.at[k, j - 1], to),
-                remote(zs_send.at[k], zs_recv.at[k, j - 1], zss_sem.at[k, j - 1],
-                       zsr_sem.at[k, j - 1], to))
+        to = y_peer + (z_peer - y_peer) * swapped(k)
+        return (remote(y_send.at[k], y_recv.at[k], yds_sem.at[k], ydr_sem.at[k], to),
+                remote(ys_send.at[k], ys_recv.at[k], yss_sem.at[k], ysr_sem.at[k], to))
+
+    def z_copies(k):
+        to = z_peer + (y_peer - z_peer) * swapped(k)
+        return (remote(z_send.at[k, 1 - second(k)], z_recv.at[k], zds_sem.at[k], zdr_sem.at[k], to),
+                remote(zs_send.at[k], zs_recv.at[k], zss_sem.at[k], zsr_sem.at[k], to))
+
+    def w_copies(k):
+        return (remote(w_send.at[k, 1 - far], w_recv.at[k], wds_sem.at[k], wdr_sem.at[k], w_peer),
+                remote(ws_send.at[k], ws_recv.at[k], wss_sem.at[k], wsr_sem.at[k], w_peer))
 
     squares[...] = jnp.zeros_like(squares)
 
@@ -148,18 +168,18 @@
         def _():
             k = t
             load(k).wait()
-            theirs = g_ref[pl.ds(pl.multiple_of((1 - core) * half, half), half), :]
+            theirs = g_ref[swapped(k), pl.ds(pl.multiple_of((1 - core) * half, half), half), :]
             c_send[k] = jnp.dot(theirs, p_buf[k], preferred_element_type=jnp.float32)
             core_copy(k).start()
 
         @pl.when(jnp.logical_and(t >= 1, t < chunks + 1))
         def _():
             k = t - 1
-            away = pl.multiple_of((1 - y) * quarter, quarter)
-            home = pl.multiple_of(y * quarter, quarter)
+            away = pl.multiple_of((1 - first(k)) * quarter, quarter)
+            home = pl.multiple_of(first(k) * quarter, quarter)
             base = core * half
-            g_away = g_ref[pl.ds(pl.multiple_of(base + away, quarter), quarter), :]
-            g_home = g_ref[pl.ds(pl.multiple_of(base + home, quarter), quarter), :]
+            g_away = g_ref[swapped(k), pl.ds(pl.multiple_of(base + away, quarter), quarter), :]
+            g_home = g_ref[swapped(k), pl.ds(pl.multiple_of(base + home, quarter), quarter), :]
             d_away = jnp.dot(g_away, p_buf[k], preferred_element_type=jnp.float32)
             d_home = jnp.dot(g_home, p_buf[k], preferred_element_type=jnp.float32)
             core_copy(k).wait_recv()
@@ -179,31 +199,43 @@
             scale = to_rows(ys_recv[k])[:, 0:1]
             v = y_own[k] + y_recv[k].astype(jnp.int32).astype(jnp.float32) * scale
             top = row_scale(v)
-            q = to_int16(v, top)
-            z_send[k] = q.reshape(zs, rows, width)
+            z_send[k] = to_int16(v, top).reshape(2, eighth, width)
             zs_send[k] = to_lanes(top)
-            for j in range(1, zs):
-                for c in z_copies(k, j):
-                    c.start()
-            y_own[k] = v
-            acc[k] = y_own[k, pl.ds(pl.multiple_of(z * rows, rows), rows), :]
-
-        @pl.when(t >= 5)
+            for c in z_copies(k):
+                c.start()
+            z_own[k] = v.reshape(2, eighth, width)
+
+        @pl.when(jnp.logical_and(t >= 5, t < chunks + 5))
         def _():
             k = t - 5
-            v = acc[k]
-            for j in range(1, zs):
-                for c in z_copies(k, j):
-                    c.wait_recv()
-                turned[...] = to_rows(zs_recv[k, j - 1])
-                scale = turned[pl.ds(pl.multiple_of(z * rows, rows), rows), :][:, 0:1]
-                v = v + z_recv[k, j - 1].astype(jnp.int32).astype(jnp.float32) * scale
+            for c in z_copies(k):
+                c.wait_recv()
+            turned[...] = to_rows(zs_recv[k])
+            at = pl.multiple_of(second(k) * eighth, eighth)
+            scale = turned[pl.ds(at, eighth), :][:, 0:1]
+            v = z_own[k, second(k)] + z_recv[k].astype(jnp.int32).astype(jnp.float32) * scale
+            top = row_scale(v)
+            w_send[k] = to_int16(v, top).reshape(2, rows, width)
+            ws_send[k] = to_lanes(jnp.concatenate([top, top], axis=0))
+            for c in w_copies(k):
+                c.start()
+            z_own[k, 0] = v
+            acc[k] = z_own[k, 0, pl.ds(pl.multiple_of(far * rows, rows), rows), :]
+
+        @pl.when(t >= 7)
+        def _():
+            k = t - 7
+            for c in w_copies(k):
+                c.wait_recv()
+            turned[...] = to_rows(ws_recv[k])
+            scale = turned[pl.ds(pl.multiple_of(far * rows, rows), rows), :][:, 0:1]
+            v = acc[k] + w_recv[k].astype(jnp.int32).astype(jnp.float32) * scale
             acc[k] = v
             squares[...] += jnp.sum(v * v, axis=1, keepdims=True)
 
         return carry
 
-    lax.fori_loop(0, chunks + 5, step, 0)
+    lax.fori_loop(0, chunks + 7, step, 0)
 
     factor = lax.rsqrt(squares[...] + epsilon)[:, 0:1]
     for k in range(chunks):
@@ -223,9 +255,10 @@
         core_copy(k).wait_send()
         for c in y_copies(k):
             c.wait_send()
-        for j in range(1, zs):
-            for c in z_copies(k, j):
-                c.wait_send()
+        for c in z_copies(k):
+            c.wait_send()
+        for c in w_copies(k):
+            c.wait_send()
         return carry
 
     lax.fori_loop(0, chunks, drain, 0)
@@ -278,10 +311,11 @@
         left = jnp.zeros((TRAIN_PER, VAL), jnp.float32)
         for a in range(TRAIN_TASKS):
             left = left + jnp.where(pairs_ref[i, 0] == a, whole_gram[a], 0.0)
-        chosen = ones_where(number((VAL, VAL_PER), 0)
-                            == number((VAL, VAL_PER), 1) + pairs_ref[i, 1] * VAL_PER)
-        tile_ref[i] = jnp.dot(left, chosen, preferred_element_type=jnp.float32,
-                              precision=lax.Precision.HIGHEST)
+        chosen = ones_where(number((VAL_PER, VAL), 1)
+                            == number((VAL_PER, VAL), 0) + pairs_ref[i, 1] * VAL_PER)
+        tile_ref[i] = lax.dot_general(chosen, left, (((1,), (1,)), ((), ())),
+                                      preferred_element_type=jnp.float32,
+                                      precision=lax.Precision.HIGHEST)
 
 
 def project(n, gradients, proj_matrix, train_task, val_task, task_pairs, owner_slot):
@@ -298,13 +332,13 @@
     return pl.pallas_call(
         functools.partial(kernel, zs),
         out_shape=(jax.ShapeDtypeStruct((rows, cols), bf16),
-                   jax.ShapeDtypeStruct((pairs, TRAIN_PER, VAL_PER), f32),
+                   jax.ShapeDtypeStruct((pairs, VAL_PER, TRAIN_PER), f32),
                    jax.ShapeDtypeStruct((1, total), f32)),
         in_specs=[pl.BlockSpec(memory_space=pltpu.SMEM), vmem, vmem, vmem, vmem,
                   pl.BlockSpec(memory_space=pl.ANY)],
         out_specs=(vmem, vmem, vmem),
         scratch_shapes=[
-            pltpu.VMEM((total, depth), bf16),
+            pltpu.VMEM((2, total, depth), bf16),
             pltpu.VMEM((total, total), bf16),
             pltpu.VMEM((n, part, VAL), f32),
             pltpu.VMEM((16, VAL), f32),
@@ -317,10 +351,15 @@
             pltpu.VMEM((chunks, quarter, width), i16),
             pltpu.VMEM((chunks, 1, quarter), f32),
             pltpu.VMEM((chunks, 1, quarter), f32),
-            pltpu.VMEM((chunks, zs, rows, width), i16),
-            pltpu.VMEM((chunks, zs - 1, rows, width), i16),
-            pltpu.VMEM((chunks, 1, quarter), f32),
-            pltpu.VMEM((chunks, zs - 1, 1, quarter), f32),
+            pltpu.VMEM((chunks, 2, quarter // 2, width), f32),
+            pltpu.VMEM((chunks, 2, quarter // 2, width), i16),
+            pltpu.VMEM((chunks, quarter // 2, width), i16),
+            pltpu.VMEM((chunks, 1, quarter), f32),
+            pltpu.VMEM((chunks, 1, quarter), f32),
+            pltpu.VMEM((chunks, 2, rows, width), i16),
+            pltpu.VMEM((chunks, rows, width), i16),
+            pltpu.VMEM((chunks, 1, quarter), f32),
+            pltpu.VMEM((chunks, 1, quarter), f32),
             pltpu.VMEM((chunks, rows, width), f32),
             pltpu.VMEM((rows, 128), f32),
             pltpu.VMEM((128, 128), f32),
@@ -332,8 +371,8 @@
             dma((chunks,)),
             dma((chunks,)), dma((chunks,)),
             dma((chunks,)), dma((chunks,)), dma((chunks,)), dma((chunks,)),
-            dma((chunks, zs - 1)), dma((chunks, zs - 1)),
-            dma((chunks, zs - 1)), dma((chunks, zs - 1)),
+            dma((chunks,)), dma((chunks,)), dma((chunks,)), dma((chunks,)),
+            dma((chunks,)), dma((chunks,)), dma((chunks,)), dma((chunks,)),
             dma((n - 1,)), dma((n - 1,)), dma((n - 1,)), dma((n - 1,)),
             dma((n - 1,)), dma((n - 1,)), dma((n - 1,)), dma((n - 1,)),
         ],
@@ -341,7 +380,7 @@
             collective_id=0, has_side_effects=True, vmem_limit_bytes=60 * 2**20),
         cost_estimate=pl.CostEstimate(
             flops=2 * total * depth * cols, bytes_accessed=2 * depth * cols, transcendentals=0),
-    )(task_pairs, gradients, owner_slot.reshape(1, -1), train_task.reshape(1, -1),
+    )(task_pairs, gradients, owner_slot.reshape(1, -1), train_task.reshape(-1, 128),
       val_task.reshape(1, -1), proj_matrix)
 
 
@@ -350,7 +389,7 @@
     unit_rows, tiles, scores = project(
         n, gradients, proj_matrix, train_task, val_task, task_pairs, owner_slot)
     mine = lax.dynamic_slice(scores, (0, lax.axis_index("param") * rows), (1, rows))
-    return (unit_rows, tiles, mine.reshape(rows))
+    return (unit_rows, tiles.transpose(0, 2, 1), mine.reshape(rows))
 
 
 def shards(gradients, proj_matrix, train_task, val_task, task_pairs, owner_slot):

time: 99 us -> 96.7 us (0.977)
  local copies, waits for them, and re-layouts: 5.77 us -> 4.45 us
  Pallas kernels: 92.3 us -> 91.2 us
    reshape x2 -> x1, local copies, waits for them, and re-layouts: 2.47 us -> 1.26 us  [fused(): return (unit_rows, tiles.transpose(0, 2, 1), mine.reshape(rows))]
    pallas_call x1, Pallas kernels: 92.3 us -> 91.2 us  [project(): pl.pallas_call(functools.partial(kernel, zs), out_shape=(jax.ShapeDtypeSt...]
where the time goes in v3:
time: 96.7 us; the launch traced here: 96.3 us
  Pallas kernels  91.2 us (94%)
  local copies, waits for them, and re-layouts  4.45 us (5%)
    pallas_call x1, Pallas kernels, project(): pl.pallas_call(functools.partial(kernel, zs), out_shape=(jax.ShapeDtypeSt...  91.2 us
    unnamed x2, local copies, waits for them, and re-layouts  3.19 us

profile of v3, /device:TPU:0, one launch (start us, length us, event | category | flops | bytes accessed | tf_op | source)
XLA Modules:
  0.0 96.3 jit_solution(5982110993912917976)
XLA Ops:
  0.6 91.2 %shard_map.85 = (bf16[32,8192]{1,0:T(8,128)(2,1)}, f32[2,16,32]{2,1,0:T(8,128)}, f32[1,512]{1,0:T(1,128)}) custom-call(s32[2,2]{1,0:T(2,128)} %pairs_ref.1, bf16[512,640]{1,0:T(8,128)(2,1)} %g_in.1, s32[1,512]{1,0:T(1,128)} %bitcast.7, s32[3,128]{1,0:T(4,128)} %bitcast.8, s32[1,128]{1,0:T(1,128)} %bitcast.9, bf16[640,8192]{1,0:T(8,128)(2,1)} %p_ref.1), custom_call_target="tpu_custom_call" | custom-call | flops 5368709120 | bytes 10485760 | tf_op jit(solution)/shard_map/pallas_call | solution.py:332
  91.8 1.3 %dynamic-slice_bitcast_fusion = f32[32]{0:T(128)} fusion(f32[1,512]{1,0:T(1,128)} %get-tuple-element.8, s32[]{:T(128)S(6)} %select_n.3), kind=kLoop, calls=%fused_computation | loop fusion | bytes 260 | tf_op jit(solution)/shard_map/reshape | solution.py:392
  93.1 1.9 %copy.11 = bf16[32,8192]{1,0:T(8,128)(2,1)} copy(bf16[32,8192]{1,0:T(8,128)(2,1)} %get-tuple-element.12) | data formatting | bytes 1048576
  95.0 1.3 %copy.12 = f32[2,32,16]{1,2,0:T(8,128)} copy(f32[2,32,16]{1,2,0:T(8,128)} %bitcast.6) | data formatting | bytes 8192
